TPU v7x, 512 devices: a whole 4x8x8 slice. The times are simulated.
512 devices in a mesh: dom: 128 (over z, y, core), sub: 4 (over x).
Axes of the slice: x: 4, y: 8, z: 8, core: 2. Of those that a mesh axis runs over, the one named last changes fastest.
Arguments:
- rhs: float32 [64, 8, 65536], P(None, None, ('dom', 'sub')), may hold values from -6 to 6
- guess: float32 [64, 8, 65536], P(None, None, ('dom', 'sub')), may hold values from -4 to 4
- diag_blocks: bfloat16 [2, 64, 64], replicated
- face_blocks: bfloat16 [6, 2, 64, 64], replicated, may hold values from -0.3125 to 0.3125
- smoother: bfloat16 [2, 64, 64], replicated
- coarse_inverse: bfloat16 [64, 64], replicated
- elem_type: int32 [65536], P(('dom', 'sub')), may hold values from 0 to 1
- face_type: int32 [6, 65536], P(None, ('dom', 'sub')), may hold values from 0 to 1
- neighbours: int32 [6, 65536], P(None, ('dom', 'sub')), may hold values from 0 to 239, as said below
- send_near: int32 [2, 16384], P(None, ('dom', 'sub')), may hold values from 0 to 127
- send_far: int32 [2, 4096], P(None, ('dom', 'sub')), may hold values from 0 to 127
- sub_send: int32 [4096], P(('dom', 'sub')), may hold values from 0 to 127
- partner: int32 [65536], P(('dom', 'sub')), may hold values from 0 to 143, as said below
- pair_send: int32 [8192], P(('dom', 'sub')), may hold values from 0 to 127, as said below
Outputs:
- solution: float32 [64, 8, 65536], P(None, None, ('dom', 'sub'))
- residual: float32 [64, 8, 65536], P(None, None, ('dom', 'sub'))
Inputs may be any that keep to these rules, and one draw needn't show every extreme that they name: `neighbours`: values below 128 are the device's own elements; the rest index its 112 received rows in the order of the first step. On each device the partner relation is mutual: local values pair two distinct local elements with each other; each value 128 + q for q below 16 appears exactly once, and the element holding it is entry q of the device's pair_send. `pair_send`: on each device the 16 entries are distinct; slot q pairs with slot q of the device whose sub index differs in the lowest bit.
All inputs are finite; a program needn't handle non-finite values.
Results may differ from a plain program's by a relative error of at most 0.012.
Values may be sent and summed in bfloat16 or wider, within the bound.
No kernel may reach another device: no remote copies, remote signals or barrier semaphores. Data moves between devices by JAX's collectives and lax.ppermute only.
A program may use at most 64 MiB of HBM per device.

v0:
```python
import jax
import jax.numpy as jnp
from jax import lax
from jax.sharding import PartitionSpec as P

SWEEPS = 2


def from_behind(array, axis, by):
    peers = lax.axis_size(axis)
    pairs = [(i, i + by) for i in range(peers) if 0 <= i + by < peers]
    return lax.ppermute(array, axis, pairs)


def partner_2(block, axis, stride):
    count = lax.axis_size(axis)
    route = []
    for low in range(count):
        high = low | 1 << stride
        if high != low and high < count:
            route += [(low, high), (high, low)]
    return lax.ppermute(block, axis, route)


def stack_apply(blocks, field_b, kinds):
    variants = blocks.shape[0]
    node_rows, rhs_width, elements = field_b.shape
    blank = jnp.zeros_like(field_b)
    pieces = [
        jnp.where(kinds[None, None, :] == variant, field_b, blank) for variant in range(variants)
    ]
    operand = jnp.concatenate(pieces, axis=0).reshape(variants * node_rows, rhs_width * elements)
    wide_blocks = jnp.concatenate([blocks[variant] for variant in range(variants)], axis=1)
    product = jnp.dot(wide_blocks, operand, preferred_element_type=jnp.float32)
    return product.reshape(node_rows, rhs_width, elements)


def body(
    rhs,
    guess,
    diag_blocks,
    face_blocks,
    smoother,
    coarse_inverse,
    elem_type,
    face_type,
    neighbours,
    send_near,
    send_far,
    sub_send,
    partner,
    pair_send,
):

    def apply_local(field_b):
        up_near = jnp.take(field_b, send_near[1], axis=2)
        down_near = jnp.take(field_b, send_near[0], axis=2)
        up_far = jnp.take(field_b, send_far[1], axis=2)
        down_far = jnp.take(field_b, send_far[0], axis=2)
        from_below = from_behind(up_near, "dom", 1)
        from_above = from_behind(down_near, "dom", -1)
        far_below = from_behind(up_far, "dom", 2)
        far_above = from_behind(down_far, "dom", -2)
        side_rows = lax.all_gather(jnp.take(field_b, sub_send, axis=2), "sub", axis=2, tiled=True)
        extended = jnp.concatenate(
            [field_b, from_below, from_above, far_below, far_above, side_rows], axis=2
        )
        total = stack_apply(diag_blocks, field_b, elem_type)
        for face_index in range(6):
            beside = jnp.take(extended, neighbours[face_index], axis=2)
            total = total + stack_apply(face_blocks[face_index], beside, face_type[face_index])
        return total

    iterate = guess
    for rounds in range(SWEEPS):
        sweep_res = rhs - apply_local(iterate.astype(jnp.bfloat16))
        iterate = iterate + stack_apply(smoother, sweep_res.astype(jnp.bfloat16), elem_type)
    residual = rhs - apply_local(iterate.astype(jnp.bfloat16))
    outgoing = jnp.take(residual, pair_send, axis=2)
    incoming = partner_2(outgoing.astype(jnp.bfloat16), "sub", 0).astype(outgoing.dtype)
    joined = jnp.concatenate([residual, incoming], axis=2)
    coarse = residual + jnp.take(joined, partner, axis=2)
    node_rows, rhs_width, elements = coarse.shape
    coarse_b = coarse.astype(jnp.bfloat16).reshape(node_rows, rhs_width * elements)
    update = jnp.dot(coarse_inverse, coarse_b, preferred_element_type=jnp.float32)
    solution = iterate + update.reshape(node_rows, rhs_width, elements)
    return (solution, residual)


def solution(mesh):
    in_specs = (
        P(None, None, ("dom", "sub")),
        P(None, None, ("dom", "sub")),
        P(),
        P(),
        P(),
        P(),
        P(("dom", "sub")),
        P(None, ("dom", "sub")),
        P(None, ("dom", "sub")),
        P(None, ("dom", "sub")),
        P(None, ("dom", "sub")),
        P(("dom", "sub")),
        P(("dom", "sub")),
        P(("dom", "sub")),
    )
    out_specs = (P(None, None, ("dom", "sub")), P(None, None, ("dom", "sub")))
    return jax.shard_map(body, mesh=mesh, in_specs=in_specs, out_specs=out_specs, check_vma=False)
```

profile of v0, /device:TPU:256, one launch (start us, length us, event | category | flops | bytes accessed | tf_op | source)
XLA Modules:
  0.0 147.1 jit_solution(16618105193743809623)
XLA Ops:
  1.3 1.0 broadcast_select_fusion.27
  3.3 1.9 %collective-permute-start = (bf16[64,8,32]{2,0,1:T(8,128)(2,1)S(1)}, bf16[64,8,32]{2,0,1:T(8,128)(2,1)S(1)}, u32[]{:S(2)}, u32[]{:S(2)}) collective-permute-start(bf16[64,8,32]{2,0,1:T(8,128)(2,1)S(1)} %select_bitcast_fusion.5), channel_id=1, source_target_pairs={{0,4},{4,8},{8,12},{12,16},{16,20},{20,24},{24,28},{28,32},{32,36}... | collective-permute-start | bytes 98312 | tf_op jit(solution)/shard_map/ppermute | solution.py:12
  6.1 7.0 %collective-permute-start.1 = (bf16[64,8,32]{2,0,1:T(8,128)(2,1)S(1)}, bf16[64,8,32]{2,0,1:T(8,128)(2,1)S(1)}, u32[]{:S(2)}, u32[]{:S(2)}) collective-permute-start(bf16[64,8,32]{2,0,1:T(8,128)(2,1)S(1)} %select_bitcast_fusion.4), channel_id=1, source_target_pairs={{4,0},{8,4},{12,8},{16,12},{20,16},{24,20},{28,24},{32,28},{36,32}... | collective-permute-start | bytes 98312 | tf_op jit(solution)/shard_map/ppermute | solution.py:12
  13.7 1.9 %collective-permute-start.2 = (bf16[64,8,8]{0,1,2:T(8,128)(2,1)S(1)}, bf16[64,8,8]{0,1,2:T(8,128)(2,1)S(1)}, u32[]{:S(2)}, u32[]{:S(2)}) collective-permute-start(bf16[64,8,8]{0,1,2:T(8,128)(2,1)S(1)} %select_bitcast_fusion.14), channel_id=1, source_target_pairs={{0,8},{4,12},{8,16},{12,20},{16,24},{20,28},{24,32},{28,36},{32,40... | collective-permute-start | bytes 24584 | tf_op jit(solution)/shard_map/ppermute | solution.py:12
  16.3 7.2 %collective-permute-start.3 = (bf16[64,8,8]{0,1,2:T(8,128)(2,1)S(1)}, bf16[64,8,8]{0,1,2:T(8,128)(2,1)S(1)}, u32[]{:S(2)}, u32[]{:S(2)}) collective-permute-start(bf16[64,8,8]{0,1,2:T(8,128)(2,1)S(1)} %select_bitcast_fusion.13), channel_id=1, source_target_pairs={{8,0},{12,4},{16,8},{20,12},{24,16},{28,20},{32,24},{36,28},{40,32... | collective-permute-start | bytes 24584 | tf_op jit(solution)/shard_map/ppermute | solution.py:12
  25.6 12.2 %all_gather.9 = bf16[64,8,32]{0,1,2:T(8,128)(2,1)S(1)} all-gather(bf16[64,8,8]{0,1,2:T(8,128)(2,1)S(1)} %select_bitcast_fusion.12), channel_id=1, replica_groups=mesh['dom'=128,'sub'=4] {'sub'}, dimensions={2}, use_global_device_ids=true | all-gather | bytes 40960 | tf_op jit(solution)/shard_map/all_gather | solution.py:64
  40.0 0.7 gather_fusion.8
  43.4 0.7 gather_fusion.11
  48.2 0.7 copy-done.2
  52.9 1.9 %collective-permute-start.4 = (bf16[64,8,32]{2,0,1:T(8,128)(2,1)S(1)}, bf16[64,8,32]{2,0,1:T(8,128)(2,1)S(1)}, u32[]{:S(2)}, u32[]{:S(2)}) collective-permute-start(bf16[64,8,32]{2,0,1:T(8,128)(2,1)S(1)} %select_bitcast_fusion.3), channel_id=1, source_target_pairs={{0,4},{4,8},{8,12},{12,16},{16,20},{20,24},{24,28},{28,32},{32,36}... | collective-permute-start | bytes 98312 | tf_op jit(solution)/shard_map/ppermute | solution.py:12
  55.0 7.0 %collective-permute-start.5 = (bf16[64,8,32]{2,0,1:T(8,128)(2,1)S(1)}, bf16[64,8,32]{2,0,1:T(8,128)(2,1)S(1)}, u32[]{:S(2)}, u32[]{:S(2)}) collective-permute-start(bf16[64,8,32]{2,0,1:T(8,128)(2,1)S(1)} %select_bitcast_fusion.2), channel_id=1, source_target_pairs={{4,0},{8,4},{12,8},{16,12},{20,16},{24,20},{28,24},{32,28},{36,32}... | collective-permute-start | bytes 98312 | tf_op jit(solution)/shard_map/ppermute | solution.py:12
  62.1 1.9 %collective-permute-start.6 = (bf16[64,8,8]{0,1,2:T(8,128)(2,1)S(1)}, bf16[64,8,8]{0,1,2:T(8,128)(2,1)S(1)}, u32[]{:S(2)}, u32[]{:S(2)}) collective-permute-start(bf16[64,8,8]{0,1,2:T(8,128)(2,1)S(1)} %select_bitcast_fusion.11), channel_id=1, source_target_pairs={{0,8},{4,12},{8,16},{12,20},{16,24},{20,28},{24,32},{28,36},{32,40... | collective-permute-start | bytes 24584 | tf_op jit(solution)/shard_map/ppermute | solution.py:12
  64.1 7.2 %collective-permute-start.7 = (bf16[64,8,8]{0,1,2:T(8,128)(2,1)S(1)}, bf16[64,8,8]{0,1,2:T(8,128)(2,1)S(1)}, u32[]{:S(2)}, u32[]{:S(2)}) collective-permute-start(bf16[64,8,8]{0,1,2:T(8,128)(2,1)S(1)} %select_bitcast_fusion.10), channel_id=1, source_target_pairs={{8,0},{12,4},{16,8},{20,12},{24,16},{28,20},{32,24},{36,28},{40,32... | collective-permute-start | bytes 24584 | tf_op jit(solution)/shard_map/ppermute | solution.py:12
  71.4 12.0 %all_gather.10 = bf16[64,8,32]{0,1,2:T(8,128)(2,1)S(1)} all-gather(bf16[64,8,8]{0,1,2:T(8,128)(2,1)S(1)} %select_bitcast_fusion.9), channel_id=1, replica_groups=mesh['dom'=128,'sub'=4] {'sub'}, dimensions={2}, use_global_device_ids=true | all-gather | bytes 40960 | tf_op jit(solution)/shard_map/all_gather | solution.py:64
  97.1 1.9 %collective-permute-start.8 = (bf16[64,8,32]{2,0,1:T(8,128)(2,1)S(1)}, bf16[64,8,32]{2,0,1:T(8,128)(2,1)S(1)}, u32[]{:S(2)}, u32[]{:S(2)}) collective-permute-start(bf16[64,8,32]{2,0,1:T(8,128)(2,1)S(1)} %select_bitcast_fusion.1), channel_id=1, source_target_pairs={{0,4},{4,8},{8,12},{12,16},{16,20},{20,24},{24,28},{28,32},{32,36}... | collective-permute-start | bytes 98312 | tf_op jit(solution)/shard_map/ppermute | solution.py:12
  99.2 7.0 %collective-permute-start.9 = (bf16[64,8,32]{2,0,1:T(8,128)(2,1)S(1)}, bf16[64,8,32]{2,0,1:T(8,128)(2,1)S(1)}, u32[]{:S(2)}, u32[]{:S(2)}) collective-permute-start(bf16[64,8,32]{2,0,1:T(8,128)(2,1)S(1)} %select_bitcast_fusion), channel_id=1, source_target_pairs={{4,0},{8,4},{12,8},{16,12},{20,16},{24,20},{28,24},{32,28},{36,32}... | collective-permute-start | bytes 98312 | tf_op jit(solution)/shard_map/ppermute | solution.py:12
  106.3 1.9 %collective-permute-start.10 = (bf16[64,8,8]{0,1,2:T(8,128)(2,1)S(1)}, bf16[64,8,8]{0,1,2:T(8,128)(2,1)S(1)}, u32[]{:S(2)}, u32[]{:S(2)}) collective-permute-start(bf16[64,8,8]{0,1,2:T(8,128)(2,1)S(1)} %select_bitcast_fusion.8), channel_id=1, source_target_pairs={{0,8},{4,12},{8,16},{12,20},{16,24},{20,28},{24,32},{28,36},{32,40... | collective-permute-start | bytes 24584 | tf_op jit(solution)/shard_map/ppermute | solution.py:12
  108.3 7.2 %collective-permute-start.11 = (bf16[64,8,8]{0,1,2:T(8,128)(2,1)S(1)}, bf16[64,8,8]{0,1,2:T(8,128)(2,1)S(1)}, u32[]{:S(2)}, u32[]{:S(2)}) collective-permute-start(bf16[64,8,8]{0,1,2:T(8,128)(2,1)S(1)} %select_bitcast_fusion.7), channel_id=1, source_target_pairs={{8,0},{12,4},{16,8},{20,12},{24,16},{28,20},{32,24},{36,28},{40,32... | collective-permute-start | bytes 24584 | tf_op jit(solution)/shard_map/ppermute | solution.py:12
  115.6 11.9 %all_gather.11 = bf16[64,8,32]{0,1,2:T(8,128)(2,1)S(1)} all-gather(bf16[64,8,8]{0,1,2:T(8,128)(2,1)S(1)} %select_bitcast_fusion.6), channel_id=1, replica_groups=mesh['dom'=128,'sub'=4] {'sub'}, dimensions={2}, use_global_device_ids=true | all-gather | bytes 40960 | tf_op jit(solution)/shard_map/all_gather | solution.py:64
  137.9 3.1 %collective-permute-start.12 = (bf16[64,8,16]{2,0,1:T(8,128)(2,1)S(1)}, bf16[64,8,16]{2,0,1:T(8,128)(2,1)S(1)}, u32[]{:S(2)}, u32[]{:S(2)}) collective-permute-start(bf16[64,8,16]{2,0,1:T(8,128)(2,1)S(1)} %fusion.32), channel_id=1, source_target_pairs={{0,1},{1,0},{2,3},{3,2},{4,5},{5,4},{6,7},{7,6},{8,9},{9,8},{10,11... | collective-permute-start | bytes 49160 | tf_op jit(solution)/shard_map/ppermute | solution.py:22
  140.9 0.9 copy.358
  141.8 2.9 %collective-permute-done.12 = bf16[64,8,16]{2,0,1:T(8,128)(2,1)S(1)} collective-permute-done((bf16[64,8,16]{2,0,1:T(8,128)(2,1)S(1)}, bf16[64,8,16]{2,0,1:T(8,128)(2,1)S(1)}, u32[]{:S(2)}, u32[]{:S(2)}) %collective-permute-start.12) | collective-permute-done | bytes 16416 | tf_op jit(solution)/shard_map/ppermute | solution.py:22
  145.1 0.8 gather_fusion.1
  146.3 0.9 copy.357
  (249 shorter events, 43.2 us)
Async XLA Ops:
  0.6 145.4 %copy-start = (bf16[64,64]{1,0:T(8,128)(2,1)S(1)}, bf16[64,64]{1,0:T(8,128)(2,1)}, u32[]{:S(2)}) copy-start(bf16[64,64]{1,0:T(8,128)(2,1)} %param.25) | copy-start | bytes 24580
  0.6 1.9 %copy-start.8 = (s32[2,32]{1,0:T(2,128)S(1)}, s32[2,32]{1,0:T(2,128)}, u32[]{:S(2)}) copy-start(s32[2,32]{1,0:T(2,128)} %param.29) | copy-start | bytes 772
  3.2 9.9 %copy-start.9 = (s32[2,8]{1,0:T(2,128)S(1)}, s32[2,8]{1,0:T(2,128)}, u32[]{:S(2)}) copy-start(s32[2,8]{1,0:T(2,128)} %param.30) | copy-start | bytes 196
  3.3 34.9 %collective-permute-start = (bf16[64,8,32]{2,0,1:T(8,128)(2,1)S(1)}, bf16[64,8,32]{2,0,1:T(8,128)(2,1)S(1)}, u32[]{:S(2)}, u32[]{:S(2)}) collective-permute-start(bf16[64,8,32]{2,0,1:T(8,128)(2,1)S(1)} %select_bitcast_fusion.5), channel_id=1, source_target_pairs={{0,4},{4,8},{8,12},{12,16},{16,20},{20,24},{24,28},{28,32},{32,36}... | collective-permute-start | bytes 98312 | tf_op jit(solution)/shard_map/ppermute | solution.py:12
  5.9 17.7 %copy-start.10 = (s32[8]{0:T(128)S(1)}, s32[8]{0:T(128)}, u32[]{:S(2)}) copy-start(s32[8]{0:T(128)} %param.31) | copy-start | bytes 100
  5.9 17.7 %copy-start.11 = (s32[16]{0:T(128)S(1)}, s32[16]{0:T(128)}, u32[]{:S(2)}) copy-start(s32[16]{0:T(128)} %param.33) | copy-start | bytes 196
  5.9 17.7 %copy-start.12 = (s32[128]{0:T(128)S(1)}, s32[128]{0:T(128)}, u32[]{:S(2)}) copy-start(s32[128]{0:T(128)} %param.32) | copy-start | bytes 1540
  6.1 32.2 %collective-permute-start.1 = (bf16[64,8,32]{2,0,1:T(8,128)(2,1)S(1)}, bf16[64,8,32]{2,0,1:T(8,128)(2,1)S(1)}, u32[]{:S(2)}, u32[]{:S(2)}) collective-permute-start(bf16[64,8,32]{2,0,1:T(8,128)(2,1)S(1)} %select_bitcast_fusion.4), channel_id=1, source_target_pairs={{4,0},{8,4},{12,8},{16,12},{20,16},{24,20},{28,24},{32,28},{36,32}... | collective-permute-start | bytes 98312 | tf_op jit(solution)/shard_map/ppermute | solution.py:12
  13.7 24.2 %collective-permute-start.2 = (bf16[64,8,8]{0,1,2:T(8,128)(2,1)S(1)}, bf16[64,8,8]{0,1,2:T(8,128)(2,1)S(1)}, u32[]{:S(2)}, u32[]{:S(2)}) collective-permute-start(bf16[64,8,8]{0,1,2:T(8,128)(2,1)S(1)} %select_bitcast_fusion.14), channel_id=1, source_target_pairs={{0,8},{4,12},{8,16},{12,20},{16,24},{20,28},{24,32},{28,36},{32,40... | collective-permute-start | bytes 24584 | tf_op jit(solution)/shard_map/ppermute | solution.py:12
  16.3 21.8 %collective-permute-start.3 = (bf16[64,8,8]{0,1,2:T(8,128)(2,1)S(1)}, bf16[64,8,8]{0,1,2:T(8,128)(2,1)S(1)}, u32[]{:S(2)}, u32[]{:S(2)}) collective-permute-start(bf16[64,8,8]{0,1,2:T(8,128)(2,1)S(1)} %select_bitcast_fusion.13), channel_id=1, source_target_pairs={{8,0},{12,4},{16,8},{20,12},{24,16},{28,20},{32,24},{36,28},{40,32... | collective-permute-start | bytes 24584 | tf_op jit(solution)/shard_map/ppermute | solution.py:12
  23.7 1.3 copy-start.7
  23.7 1.4 copy-start.3
  23.8 1.4 copy-start.5
  46.7 1.0 copy-start.1
  48.0 1.0 copy-start.2
  52.9 30.9 %collective-permute-start.4 = (bf16[64,8,32]{2,0,1:T(8,128)(2,1)S(1)}, bf16[64,8,32]{2,0,1:T(8,128)(2,1)S(1)}, u32[]{:S(2)}, u32[]{:S(2)}) collective-permute-start(bf16[64,8,32]{2,0,1:T(8,128)(2,1)S(1)} %select_bitcast_fusion.3), channel_id=1, source_target_pairs={{0,4},{4,8},{8,12},{12,16},{16,20},{20,24},{24,28},{28,32},{32,36}... | collective-permute-start | bytes 98312 | tf_op jit(solution)/shard_map/ppermute | solution.py:12
  55.0 28.9 %collective-permute-start.5 = (bf16[64,8,32]{2,0,1:T(8,128)(2,1)S(1)}, bf16[64,8,32]{2,0,1:T(8,128)(2,1)S(1)}, u32[]{:S(2)}, u32[]{:S(2)}) collective-permute-start(bf16[64,8,32]{2,0,1:T(8,128)(2,1)S(1)} %select_bitcast_fusion.2), channel_id=1, source_target_pairs={{4,0},{8,4},{12,8},{16,12},{20,16},{24,20},{28,24},{32,28},{36,32}... | collective-permute-start | bytes 98312 | tf_op jit(solution)/shard_map/ppermute | solution.py:12
  62.1 21.5 %collective-permute-start.6 = (bf16[64,8,8]{0,1,2:T(8,128)(2,1)S(1)}, bf16[64,8,8]{0,1,2:T(8,128)(2,1)S(1)}, u32[]{:S(2)}, u32[]{:S(2)}) collective-permute-start(bf16[64,8,8]{0,1,2:T(8,128)(2,1)S(1)} %select_bitcast_fusion.11), channel_id=1, source_target_pairs={{0,8},{4,12},{8,16},{12,20},{16,24},{20,28},{24,32},{28,36},{32,40... | collective-permute-start | bytes 24584 | tf_op jit(solution)/shard_map/ppermute | solution.py:12
  64.1 19.6 %collective-permute-start.7 = (bf16[64,8,8]{0,1,2:T(8,128)(2,1)S(1)}, bf16[64,8,8]{0,1,2:T(8,128)(2,1)S(1)}, u32[]{:S(2)}, u32[]{:S(2)}) collective-permute-start(bf16[64,8,8]{0,1,2:T(8,128)(2,1)S(1)} %select_bitcast_fusion.10), channel_id=1, source_target_pairs={{8,0},{12,4},{16,8},{20,12},{24,16},{28,20},{32,24},{36,28},{40,32... | collective-permute-start | bytes 24584 | tf_op jit(solution)/shard_map/ppermute | solution.py:12
  97.1 30.8 %collective-permute-start.8 = (bf16[64,8,32]{2,0,1:T(8,128)(2,1)S(1)}, bf16[64,8,32]{2,0,1:T(8,128)(2,1)S(1)}, u32[]{:S(2)}, u32[]{:S(2)}) collective-permute-start(bf16[64,8,32]{2,0,1:T(8,128)(2,1)S(1)} %select_bitcast_fusion.1), channel_id=1, source_target_pairs={{0,4},{4,8},{8,12},{12,16},{16,20},{20,24},{24,28},{28,32},{32,36}... | collective-permute-start | bytes 98312 | tf_op jit(solution)/shard_map/ppermute | solution.py:12
  99.2 28.7 %collective-permute-start.9 = (bf16[64,8,32]{2,0,1:T(8,128)(2,1)S(1)}, bf16[64,8,32]{2,0,1:T(8,128)(2,1)S(1)}, u32[]{:S(2)}, u32[]{:S(2)}) collective-permute-start(bf16[64,8,32]{2,0,1:T(8,128)(2,1)S(1)} %select_bitcast_fusion), channel_id=1, source_target_pairs={{4,0},{8,4},{12,8},{16,12},{20,16},{24,20},{28,24},{32,28},{36,32}... | collective-permute-start | bytes 98312 | tf_op jit(solution)/shard_map/ppermute | solution.py:12
  106.3 21.3 %collective-permute-start.10 = (bf16[64,8,8]{0,1,2:T(8,128)(2,1)S(1)}, bf16[64,8,8]{0,1,2:T(8,128)(2,1)S(1)}, u32[]{:S(2)}, u32[]{:S(2)}) collective-permute-start(bf16[64,8,8]{0,1,2:T(8,128)(2,1)S(1)} %select_bitcast_fusion.8), channel_id=1, source_target_pairs={{0,8},{4,12},{8,16},{12,20},{16,24},{20,28},{24,32},{28,36},{32,40... | collective-permute-start | bytes 24584 | tf_op jit(solution)/shard_map/ppermute | solution.py:12
  108.3 19.5 %collective-permute-start.11 = (bf16[64,8,8]{0,1,2:T(8,128)(2,1)S(1)}, bf16[64,8,8]{0,1,2:T(8,128)(2,1)S(1)}, u32[]{:S(2)}, u32[]{:S(2)}) collective-permute-start(bf16[64,8,8]{0,1,2:T(8,128)(2,1)S(1)} %select_bitcast_fusion.7), channel_id=1, source_target_pairs={{8,0},{12,4},{16,8},{20,12},{24,16},{28,20},{32,24},{36,28},{40,32... | collective-permute-start | bytes 24584 | tf_op jit(solution)/shard_map/ppermute | solution.py:12
  137.9 6.9 %collective-permute-start.12 = (bf16[64,8,16]{2,0,1:T(8,128)(2,1)S(1)}, bf16[64,8,16]{2,0,1:T(8,128)(2,1)S(1)}, u32[]{:S(2)}, u32[]{:S(2)}) collective-permute-start(bf16[64,8,16]{2,0,1:T(8,128)(2,1)S(1)} %fusion.32), channel_id=1, source_target_pairs={{0,1},{1,0},{2,3},{3,2},{4,5},{5,4},{6,7},{7,6},{8,9},{9,8},{10,11... | collective-permute-start | bytes 49160 | tf_op jit(solution)/shard_map/ppermute | solution.py:22
  (2 other events, 1.5 us)
where the time goes:
time: 148 us; the launch traced here: 147 us
  starting transfers between devices  57.2 us (39%)
  local copies, waits for them, and re-layouts  39 us (26%)
  blocking collectives  36.1 us (24%)
  matrix products  6.08 us (4%)
  other arithmetic  3.72 us (3%)
  waiting for transfers between devices  2.94 us (2%)
  between operations  2.13 us (1%)
    ppermute x12, starting transfers between devices, from_behind(): return lax.ppermute(array, axis, pairs)  54.1 us
    all_gather x3, blocking collectives, apply_local(): lax.all_gather(jnp.take(field_b, sub_send, axis=2), 'sub', axis=2, tiled=...  36.1 us
    gather x36, local copies, waits for them, and re-layouts, apply_local(): beside = jnp.take(extended, neighbours[face_index], axis=2)  16.1 us
    dot_general x23, matrix products, stack_apply(): product = jnp.dot(wide_blocks, operand, preferred_element_type=jnp.float32)  5.91 us
    concatenate x23, local copies, waits for them, and re-layouts, stack_apply(): jnp.concatenate(pieces, axis=0)  4.08 us
    unnamed x28, local copies, waits for them, and re-layouts  3.7 us
    ppermute x1, starting transfers between devices, partner_2(): return lax.ppermute(block, axis, route)  3.07 us
  transfers between devices with their start and end apart: 13, of which 1 were waited for; matrix products, arithmetic and copies ran while one was open for 4% of the time, Pallas kernels for 0%

commit v1 on v0

--- a/solution.py
+++ b/solution.py
@@ -61,7 +61,12 @@
         from_above = from_behind(down_near, "dom", -1)
         far_below = from_behind(up_far, "dom", 2)
         far_above = from_behind(down_far, "dom", -2)
-        side_rows = lax.all_gather(jnp.take(field_b, sub_send, axis=2), "sub", axis=2, tiled=True)
+        side_rows = jnp.concatenate(
+            lax.all_to_all(
+                jnp.stack([jnp.take(field_b, sub_send, axis=2)] * lax.axis_size("sub")), "sub", 0, 0
+            ),
+            axis=2,
+        )
         extended = jnp.concatenate(
             [field_b, from_below, from_above, far_below, far_above, side_rows], axis=2
         )

time: 148 us -> 129 us (0.87)
  the two profiles are of different devices: /device:TPU:256 before, /device:TPU:251 now
where the time goes in v1:
time: 129 us; the launch traced here: 128 us
  starting transfers between devices  57.4 us (44%)
  local copies, waits for them, and re-layouts  41.7 us (32%)
  waiting for transfers between devices  16.8 us (13%)
  matrix products  6.09 us (5%)
  other arithmetic  3.72 us (3%)
  between operations  2.15 us (2%)
    ppermute x12, starting transfers between devices, from_behind(): return lax.ppermute(array, axis, pairs)  42.5 us
    gather x36, local copies, waits for them, and re-layouts, apply_local(): beside = jnp.take(extended, neighbours[face_index], axis=2)  16 us
    all_to_all x3, starting transfers between devices, apply_local(): lax.all_to_all(jnp.stack([jnp.take(field_b, sub_send, axis=2)] * lax.axis...  12.9 us
    ppermute x12, waiting for transfers between devices, from_behind(): return lax.ppermute(array, axis, pairs)  11.7 us
    unnamed x37, local copies, waits for them, and re-layouts  6.41 us
    dot_general x23, matrix products, stack_apply(): product = jnp.dot(wide_blocks, operand, preferred_element_type=jnp.float32)  5.92 us
    concatenate x23, local copies, waits for them, and re-layouts, stack_apply(): jnp.concatenate(pieces, axis=0)  4.08 us
    ppermute x1, waiting for transfers between devices, partner_2(): return lax.ppermute(block, axis, route)  2.91 us
  transfers between devices with their start and end apart: 16, of which 5 were waited for; matrix products, arithmetic and copies ran while one was open for 7% of the time, Pallas kernels for 0%

profile of v1, /device:TPU:251, one launch (start us, length us, event | category | flops | bytes accessed | tf_op | source)
XLA Modules:
  0.0 127.8 jit_solution(15546771017347738594)
XLA Ops:
  1.3 1.0 broadcast_select_fusion.27
  3.3 5.0 %collective-permute-start = (bf16[64,8,32]{2,0,1:T(8,128)(2,1)S(1)}, bf16[64,8,32]{2,0,1:T(8,128)(2,1)S(1)}, u32[]{:S(2)}, u32[]{:S(2)}) collective-permute-start(bf16[64,8,32]{2,0,1:T(8,128)(2,1)S(1)} %select_bitcast_fusion.5), channel_id=1, source_target_pairs={{0,4},{4,8},{8,12},{12,16},{16,20},{20,24},{24,28},{28,32},{32,36}... | collective-permute-start | bytes 98312 | tf_op jit(solution)/shard_map/ppermute | solution.py:12
  9.1 1.9 %collective-permute-start.1 = (bf16[64,8,32]{2,0,1:T(8,128)(2,1)S(1)}, bf16[64,8,32]{2,0,1:T(8,128)(2,1)S(1)}, u32[]{:S(2)}, u32[]{:S(2)}) collective-permute-start(bf16[64,8,32]{2,0,1:T(8,128)(2,1)S(1)} %select_bitcast_fusion.4), channel_id=1, source_target_pairs={{4,0},{8,4},{12,8},{16,12},{20,16},{24,20},{28,24},{32,28},{36,32}... | collective-permute-start | bytes 98312 | tf_op jit(solution)/shard_map/ppermute | solution.py:12
  11.7 3.2 %collective-permute-start.2 = (bf16[64,8,8]{0,1,2:T(8,128)(2,1)S(1)}, bf16[64,8,8]{0,1,2:T(8,128)(2,1)S(1)}, u32[]{:S(2)}, u32[]{:S(2)}) collective-permute-start(bf16[64,8,8]{0,1,2:T(8,128)(2,1)S(1)} %select_bitcast_fusion.14), channel_id=1, source_target_pairs={{0,8},{4,12},{8,16},{12,20},{16,24},{20,28},{24,32},{28,36},{32,40... | collective-permute-start | bytes 24584 | tf_op jit(solution)/shard_map/ppermute | solution.py:12
  15.6 2.1 %collective-permute-start.3 = (bf16[64,8,8]{0,1,2:T(8,128)(2,1)S(1)}, bf16[64,8,8]{0,1,2:T(8,128)(2,1)S(1)}, u32[]{:S(2)}, u32[]{:S(2)}) collective-permute-start(bf16[64,8,8]{0,1,2:T(8,128)(2,1)S(1)} %select_bitcast_fusion.13), channel_id=1, source_target_pairs={{8,0},{12,4},{16,8},{20,12},{24,16},{28,20},{32,24},{36,28},{40,32... | collective-permute-start | bytes 24584 | tf_op jit(solution)/shard_map/ppermute | solution.py:12
  19.1 4.3 %all-to-all-start = ((bf16[4,2,2048]{2,1,0:T(2,128)(2,1)}), bf16[4,2,2048]{2,1,0:T(2,128)(2,1)S(1)}, u32[]{:S(2)}, u32[]{:S(2)}) async-start(bf16[4,2,2048]{2,1,0:T(2,128)(2,1)} %reshape.730), calls=%async_computation | async-start | bytes 65536 | tf_op jit(solution)/shard_map/all_to_all | solution.py:65
  25.1 1.4 %all-to-all-done = bf16[4,2,2048]{2,1,0:T(2,128)(2,1)S(1)} async-done(((bf16[4,2,2048]{2,1,0:T(2,128)(2,1)}), bf16[4,2,2048]{2,1,0:T(2,128)(2,1)S(1)}, u32[]{:S(2)}, u32[]{:S(2)}) %all-to-all-start) | async-done | bytes 32800 | tf_op jit(solution)/shard_map/all_to_all | solution.py:65
  41.5 12.3 %collective-permute-start.4 = (bf16[64,8,32]{2,0,1:T(8,128)(2,1)S(1)}, bf16[64,8,32]{2,0,1:T(8,128)(2,1)S(1)}, u32[]{:S(2)}, u32[]{:S(2)}) collective-permute-start(bf16[64,8,32]{2,0,1:T(8,128)(2,1)S(1)} %select_bitcast_fusion.3), channel_id=1, source_target_pairs={{0,4},{4,8},{8,12},{12,16},{16,20},{20,24},{24,28},{28,32},{32,36}... | collective-permute-start | bytes 98312 | tf_op jit(solution)/shard_map/ppermute | solution.py:12
  54.0 1.9 %collective-permute-start.6 = (bf16[64,8,8]{0,1,2:T(8,128)(2,1)S(1)}, bf16[64,8,8]{0,1,2:T(8,128)(2,1)S(1)}, u32[]{:S(2)}, u32[]{:S(2)}) collective-permute-start(bf16[64,8,8]{0,1,2:T(8,128)(2,1)S(1)} %select_bitcast_fusion.11), channel_id=1, source_target_pairs={{0,8},{4,12},{8,16},{12,20},{16,24},{20,28},{24,32},{28,36},{32,40... | collective-permute-start | bytes 24584 | tf_op jit(solution)/shard_map/ppermute | solution.py:12
  56.0 3.4 %collective-permute-start.7 = (bf16[64,8,8]{0,1,2:T(8,128)(2,1)S(1)}, bf16[64,8,8]{0,1,2:T(8,128)(2,1)S(1)}, u32[]{:S(2)}, u32[]{:S(2)}) collective-permute-start(bf16[64,8,8]{0,1,2:T(8,128)(2,1)S(1)} %select_bitcast_fusion.10), channel_id=1, source_target_pairs={{8,0},{12,4},{16,8},{20,12},{24,16},{28,20},{32,24},{36,28},{40,32... | collective-permute-start | bytes 24584 | tf_op jit(solution)/shard_map/ppermute | solution.py:12
  60.2 4.4 %all-to-all-start.1 = ((bf16[4,2,2048]{2,1,0:T(2,128)(2,1)}), bf16[4,2,2048]{2,1,0:T(2,128)(2,1)S(1)}, u32[]{:S(2)}, u32[]{:S(2)}) async-start(bf16[4,2,2048]{2,1,0:T(2,128)(2,1)} %reshape.732), calls=%async_computation.1 | async-start | bytes 65536 | tf_op jit(solution)/shard_map/all_to_all | solution.py:65
  64.7 2.1 %collective-permute-start.5 = (bf16[64,8,32]{2,0,1:T(8,128)(2,1)S(1)}, bf16[64,8,32]{2,0,1:T(8,128)(2,1)S(1)}, u32[]{:S(2)}, u32[]{:S(2)}) collective-permute-start(bf16[64,8,32]{2,0,1:T(8,128)(2,1)S(1)} %select_bitcast_fusion.2), channel_id=1, source_target_pairs={{4,0},{8,4},{12,8},{16,12},{20,16},{24,20},{28,24},{32,28},{36,32}... | collective-permute-start | bytes 98312 | tf_op jit(solution)/shard_map/ppermute | solution.py:12
  68.0 6.2 %collective-permute-done.5 = bf16[64,8,32]{2,0,1:T(8,128)(2,1)S(1)} collective-permute-done((bf16[64,8,32]{2,0,1:T(8,128)(2,1)S(1)}, bf16[64,8,32]{2,0,1:T(8,128)(2,1)S(1)}, u32[]{:S(2)}, u32[]{:S(2)}) %collective-permute-start.5) | collective-permute-done | bytes 32800 | tf_op jit(solution)/shard_map/ppermute | solution.py:12
  87.5 1.9 %collective-permute-start.8 = (bf16[64,8,32]{2,0,1:T(8,128)(2,1)S(1)}, bf16[64,8,32]{2,0,1:T(8,128)(2,1)S(1)}, u32[]{:S(2)}, u32[]{:S(2)}) collective-permute-start(bf16[64,8,32]{2,0,1:T(8,128)(2,1)S(1)} %select_bitcast_fusion.1), channel_id=1, source_target_pairs={{0,4},{4,8},{8,12},{12,16},{16,20},{20,24},{24,28},{28,32},{32,36}... | collective-permute-start | bytes 98312 | tf_op jit(solution)/shard_map/ppermute | solution.py:12
  89.6 1.9 %collective-permute-start.10 = (bf16[64,8,8]{0,1,2:T(8,128)(2,1)S(1)}, bf16[64,8,8]{0,1,2:T(8,128)(2,1)S(1)}, u32[]{:S(2)}, u32[]{:S(2)}) collective-permute-start(bf16[64,8,8]{0,1,2:T(8,128)(2,1)S(1)} %select_bitcast_fusion.8), channel_id=1, source_target_pairs={{0,8},{4,12},{8,16},{12,20},{16,24},{20,28},{24,32},{28,36},{32,40... | collective-permute-start | bytes 24584 | tf_op jit(solution)/shard_map/ppermute | solution.py:12
  91.6 3.3 %collective-permute-start.11 = (bf16[64,8,8]{0,1,2:T(8,128)(2,1)S(1)}, bf16[64,8,8]{0,1,2:T(8,128)(2,1)S(1)}, u32[]{:S(2)}, u32[]{:S(2)}) collective-permute-start(bf16[64,8,8]{0,1,2:T(8,128)(2,1)S(1)} %select_bitcast_fusion.7), channel_id=1, source_target_pairs={{8,0},{12,4},{16,8},{20,12},{24,16},{28,20},{32,24},{36,28},{40,32... | collective-permute-start | bytes 24584 | tf_op jit(solution)/shard_map/ppermute | solution.py:12
  95.8 4.2 %all-to-all-start.2 = ((bf16[4,2,2048]{2,1,0:T(2,128)(2,1)}), bf16[4,2,2048]{2,1,0:T(2,128)(2,1)S(1)}, u32[]{:S(2)}, u32[]{:S(2)}) async-start(bf16[4,2,2048]{2,1,0:T(2,128)(2,1)} %reshape.734), calls=%async_computation.2 | async-start | bytes 65536 | tf_op jit(solution)/shard_map/all_to_all | solution.py:65
  100.1 3.5 %collective-permute-start.9 = (bf16[64,8,32]{2,0,1:T(8,128)(2,1)S(1)}, bf16[64,8,32]{2,0,1:T(8,128)(2,1)S(1)}, u32[]{:S(2)}, u32[]{:S(2)}) collective-permute-start(bf16[64,8,32]{2,0,1:T(8,128)(2,1)S(1)} %select_bitcast_fusion), channel_id=1, source_target_pairs={{4,0},{8,4},{12,8},{16,12},{20,16},{24,20},{28,24},{32,28},{36,32}... | collective-permute-start | bytes 98312 | tf_op jit(solution)/shard_map/ppermute | solution.py:12
  104.2 5.5 %collective-permute-done.9 = bf16[64,8,32]{2,0,1:T(8,128)(2,1)S(1)} collective-permute-done((bf16[64,8,32]{2,0,1:T(8,128)(2,1)S(1)}, bf16[64,8,32]{2,0,1:T(8,128)(2,1)S(1)}, u32[]{:S(2)}, u32[]{:S(2)}) %collective-permute-start.9) | collective-permute-done | bytes 32800 | tf_op jit(solution)/shard_map/ppermute | solution.py:12
  119.6 1.9 %collective-permute-start.12 = (bf16[64,8,16]{2,0,1:T(8,128)(2,1)S(1)}, bf16[64,8,16]{2,0,1:T(8,128)(2,1)S(1)}, u32[]{:S(2)}, u32[]{:S(2)}) collective-permute-start(bf16[64,8,16]{2,0,1:T(8,128)(2,1)S(1)} %fusion.32), channel_id=1, source_target_pairs={{0,1},{1,0},{2,3},{3,2},{4,5},{5,4},{6,7},{7,6},{8,9},{9,8},{10,11... | collective-permute-start | bytes 49160 | tf_op jit(solution)/shard_map/ppermute | solution.py:22
  121.6 0.9 copy.367
  122.4 2.9 %collective-permute-done.12 = bf16[64,8,16]{2,0,1:T(8,128)(2,1)S(1)} collective-permute-done((bf16[64,8,16]{2,0,1:T(8,128)(2,1)S(1)}, bf16[64,8,16]{2,0,1:T(8,128)(2,1)S(1)}, u32[]{:S(2)}, u32[]{:S(2)}) %collective-permute-start.12) | collective-permute-done | bytes 16416 | tf_op jit(solution)/shard_map/ppermute | solution.py:22
  125.7 0.8 gather_fusion.1
  126.9 0.9 copy.366
  (267 shorter events, 48.8 us)
Async XLA Ops:
  0.6 126.1 %copy-start = (bf16[64,64]{1,0:T(8,128)(2,1)S(1)}, bf16[64,64]{1,0:T(8,128)(2,1)}, u32[]{:S(2)}) copy-start(bf16[64,64]{1,0:T(8,128)(2,1)} %param.25) | copy-start | bytes 24580
  0.6 1.9 %copy-start.8 = (s32[2,32]{1,0:T(2,128)S(1)}, s32[2,32]{1,0:T(2,128)}, u32[]{:S(2)}) copy-start(s32[2,32]{1,0:T(2,128)} %param.29) | copy-start | bytes 772
  3.2 7.9 %copy-start.9 = (s32[2,8]{1,0:T(2,128)S(1)}, s32[2,8]{1,0:T(2,128)}, u32[]{:S(2)}) copy-start(s32[2,8]{1,0:T(2,128)} %param.30) | copy-start | bytes 196
  3.3 23.5 %collective-permute-start = (bf16[64,8,32]{2,0,1:T(8,128)(2,1)S(1)}, bf16[64,8,32]{2,0,1:T(8,128)(2,1)S(1)}, u32[]{:S(2)}, u32[]{:S(2)}) collective-permute-start(bf16[64,8,32]{2,0,1:T(8,128)(2,1)S(1)} %select_bitcast_fusion.5), channel_id=1, source_target_pairs={{0,4},{4,8},{8,12},{12,16},{16,20},{20,24},{24,28},{28,32},{32,36}... | collective-permute-start | bytes 98312 | tf_op jit(solution)/shard_map/ppermute | solution.py:12
  8.9 8.8 %copy-start.10 = (s32[8]{0:T(128)S(1)}, s32[8]{0:T(128)}, u32[]{:S(2)}) copy-start(s32[8]{0:T(128)} %param.31) | copy-start | bytes 100
  9.1 17.7 %collective-permute-start.1 = (bf16[64,8,32]{2,0,1:T(8,128)(2,1)S(1)}, bf16[64,8,32]{2,0,1:T(8,128)(2,1)S(1)}, u32[]{:S(2)}, u32[]{:S(2)}) collective-permute-start(bf16[64,8,32]{2,0,1:T(8,128)(2,1)S(1)} %select_bitcast_fusion.4), channel_id=1, source_target_pairs={{4,0},{8,4},{12,8},{16,12},{20,16},{24,20},{28,24},{32,28},{36,32}... | collective-permute-start | bytes 98312 | tf_op jit(solution)/shard_map/ppermute | solution.py:12
  11.1 12.3 %copy-start.11 = (s32[16]{0:T(128)S(1)}, s32[16]{0:T(128)}, u32[]{:S(2)}) copy-start(s32[16]{0:T(128)} %param.33) | copy-start | bytes 196
  11.1 12.3 %copy-start.12 = (s32[128]{0:T(128)S(1)}, s32[128]{0:T(128)}, u32[]{:S(2)}) copy-start(s32[128]{0:T(128)} %param.32) | copy-start | bytes 1540
  11.7 13.1 %collective-permute-start.2 = (bf16[64,8,8]{0,1,2:T(8,128)(2,1)S(1)}, bf16[64,8,8]{0,1,2:T(8,128)(2,1)S(1)}, u32[]{:S(2)}, u32[]{:S(2)}) collective-permute-start(bf16[64,8,8]{0,1,2:T(8,128)(2,1)S(1)} %select_bitcast_fusion.14), channel_id=1, source_target_pairs={{0,8},{4,12},{8,16},{12,20},{16,24},{20,28},{24,32},{28,36},{32,40... | collective-permute-start | bytes 24584 | tf_op jit(solution)/shard_map/ppermute | solution.py:12
  15.6 9.4 %collective-permute-start.3 = (bf16[64,8,8]{0,1,2:T(8,128)(2,1)S(1)}, bf16[64,8,8]{0,1,2:T(8,128)(2,1)S(1)}, u32[]{:S(2)}, u32[]{:S(2)}) collective-permute-start(bf16[64,8,8]{0,1,2:T(8,128)(2,1)S(1)} %select_bitcast_fusion.13), channel_id=1, source_target_pairs={{8,0},{12,4},{16,8},{20,12},{24,16},{28,20},{32,24},{36,28},{40,32... | collective-permute-start | bytes 24584 | tf_op jit(solution)/shard_map/ppermute | solution.py:12
  19.1 7.4 %all-to-all-start = ((bf16[4,2,2048]{2,1,0:T(2,128)(2,1)}), bf16[4,2,2048]{2,1,0:T(2,128)(2,1)S(1)}, u32[]{:S(2)}, u32[]{:S(2)}) async-start(bf16[4,2,2048]{2,1,0:T(2,128)(2,1)} %reshape.730), calls=%async_computation | async-start | bytes 65536 | tf_op jit(solution)/shard_map/all_to_all | solution.py:65
  23.6 1.0 copy-start.5
  35.3 1.0 copy-start.1
  41.5 26.5 %collective-permute-start.4 = (bf16[64,8,32]{2,0,1:T(8,128)(2,1)S(1)}, bf16[64,8,32]{2,0,1:T(8,128)(2,1)S(1)}, u32[]{:S(2)}, u32[]{:S(2)}) collective-permute-start(bf16[64,8,32]{2,0,1:T(8,128)(2,1)S(1)} %select_bitcast_fusion.3), channel_id=1, source_target_pairs={{0,4},{4,8},{8,12},{12,16},{16,20},{20,24},{24,28},{28,32},{32,36}... | collective-permute-start | bytes 98312 | tf_op jit(solution)/shard_map/ppermute | solution.py:12
  54.0 12.8 %collective-permute-start.6 = (bf16[64,8,8]{0,1,2:T(8,128)(2,1)S(1)}, bf16[64,8,8]{0,1,2:T(8,128)(2,1)S(1)}, u32[]{:S(2)}, u32[]{:S(2)}) collective-permute-start(bf16[64,8,8]{0,1,2:T(8,128)(2,1)S(1)} %select_bitcast_fusion.11), channel_id=1, source_target_pairs={{0,8},{4,12},{8,16},{12,20},{16,24},{20,28},{24,32},{28,36},{32,40... | collective-permute-start | bytes 24584 | tf_op jit(solution)/shard_map/ppermute | solution.py:12
  56.0 10.9 %collective-permute-start.7 = (bf16[64,8,8]{0,1,2:T(8,128)(2,1)S(1)}, bf16[64,8,8]{0,1,2:T(8,128)(2,1)S(1)}, u32[]{:S(2)}, u32[]{:S(2)}) collective-permute-start(bf16[64,8,8]{0,1,2:T(8,128)(2,1)S(1)} %select_bitcast_fusion.10), channel_id=1, source_target_pairs={{8,0},{12,4},{16,8},{20,12},{24,16},{28,20},{32,24},{36,28},{40,32... | collective-permute-start | bytes 24584 | tf_op jit(solution)/shard_map/ppermute | solution.py:12
  60.2 7.5 %all-to-all-start.1 = ((bf16[4,2,2048]{2,1,0:T(2,128)(2,1)}), bf16[4,2,2048]{2,1,0:T(2,128)(2,1)S(1)}, u32[]{:S(2)}, u32[]{:S(2)}) async-start(bf16[4,2,2048]{2,1,0:T(2,128)(2,1)} %reshape.732), calls=%async_computation.1 | async-start | bytes 65536 | tf_op jit(solution)/shard_map/all_to_all | solution.py:65
  64.7 9.6 %collective-permute-start.5 = (bf16[64,8,32]{2,0,1:T(8,128)(2,1)S(1)}, bf16[64,8,32]{2,0,1:T(8,128)(2,1)S(1)}, u32[]{:S(2)}, u32[]{:S(2)}) collective-permute-start(bf16[64,8,32]{2,0,1:T(8,128)(2,1)S(1)} %select_bitcast_fusion.2), channel_id=1, source_target_pairs={{4,0},{8,4},{12,8},{16,12},{20,16},{24,20},{28,24},{32,28},{36,32}... | collective-permute-start | bytes 98312 | tf_op jit(solution)/shard_map/ppermute | solution.py:12
  87.5 16.7 %collective-permute-start.8 = (bf16[64,8,32]{2,0,1:T(8,128)(2,1)S(1)}, bf16[64,8,32]{2,0,1:T(8,128)(2,1)S(1)}, u32[]{:S(2)}, u32[]{:S(2)}) collective-permute-start(bf16[64,8,32]{2,0,1:T(8,128)(2,1)S(1)} %select_bitcast_fusion.1), channel_id=1, source_target_pairs={{0,4},{4,8},{8,12},{12,16},{16,20},{20,24},{24,28},{28,32},{32,36}... | collective-permute-start | bytes 98312 | tf_op jit(solution)/shard_map/ppermute | solution.py:12
  89.6 14.0 %collective-permute-start.10 = (bf16[64,8,8]{0,1,2:T(8,128)(2,1)S(1)}, bf16[64,8,8]{0,1,2:T(8,128)(2,1)S(1)}, u32[]{:S(2)}, u32[]{:S(2)}) collective-permute-start(bf16[64,8,8]{0,1,2:T(8,128)(2,1)S(1)} %select_bitcast_fusion.8), channel_id=1, source_target_pairs={{0,8},{4,12},{8,16},{12,20},{16,24},{20,28},{24,32},{28,36},{32,40... | collective-permute-start | bytes 24584 | tf_op jit(solution)/shard_map/ppermute | solution.py:12
  91.6 12.1 %collective-permute-start.11 = (bf16[64,8,8]{0,1,2:T(8,128)(2,1)S(1)}, bf16[64,8,8]{0,1,2:T(8,128)(2,1)S(1)}, u32[]{:S(2)}, u32[]{:S(2)}) collective-permute-start(bf16[64,8,8]{0,1,2:T(8,128)(2,1)S(1)} %select_bitcast_fusion.7), channel_id=1, source_target_pairs={{8,0},{12,4},{16,8},{20,12},{24,16},{28,20},{32,24},{36,28},{40,32... | collective-permute-start | bytes 24584 | tf_op jit(solution)/shard_map/ppermute | solution.py:12
  95.8 8.1 %all-to-all-start.2 = ((bf16[4,2,2048]{2,1,0:T(2,128)(2,1)}), bf16[4,2,2048]{2,1,0:T(2,128)(2,1)S(1)}, u32[]{:S(2)}, u32[]{:S(2)}) async-start(bf16[4,2,2048]{2,1,0:T(2,128)(2,1)} %reshape.734), calls=%async_computation.2 | async-start | bytes 65536 | tf_op jit(solution)/shard_map/all_to_all | solution.py:65
  100.1 9.6 %collective-permute-start.9 = (bf16[64,8,32]{2,0,1:T(8,128)(2,1)S(1)}, bf16[64,8,32]{2,0,1:T(8,128)(2,1)S(1)}, u32[]{:S(2)}, u32[]{:S(2)}) collective-permute-start(bf16[64,8,32]{2,0,1:T(8,128)(2,1)S(1)} %select_bitcast_fusion), channel_id=1, source_target_pairs={{4,0},{8,4},{12,8},{16,12},{20,16},{24,20},{28,24},{32,28},{36,32}... | collective-permute-start | bytes 98312 | tf_op jit(solution)/shard_map/ppermute | solution.py:12
  119.6 5.7 %collective-permute-start.12 = (bf16[64,8,16]{2,0,1:T(8,128)(2,1)S(1)}, bf16[64,8,16]{2,0,1:T(8,128)(2,1)S(1)}, u32[]{:S(2)}, u32[]{:S(2)}) collective-permute-start(bf16[64,8,16]{2,0,1:T(8,128)(2,1)S(1)} %fusion.32), channel_id=1, source_target_pairs={{0,1},{1,0},{2,3},{3,2},{4,5},{5,4},{6,7},{7,6},{8,9},{9,8},{10,11... | collective-permute-start | bytes 49160 | tf_op jit(solution)/shard_map/ppermute | solution.py:22
  (5 other events, 4.2 us)
